TPU v7x, 256 devices: a whole 4x4x8 slice. The times are simulated.
256 devices in a mesh: src: 32 (over z, y), rcv: 8 (over x, core).
Axes of the slice: x: 4, y: 4, z: 8, core: 2. Of those that a mesh axis runs over, the one named last changes fastest.
Arguments:
- src_traces: bfloat16 [2, 8, 1024, 2048], P(None, 'rcv', 'src'), may hold values from -6 to 6
- rcv_traces: bfloat16 [2, 32, 1024, 2048], P(None, 'src', 'rcv'), may hold values from -6 to 6
- src_owner: int32 [2, 32], P(None, 'src'), may hold values from 0 to 7
- rcv_owner: int32 [2, 8], P(None, 'rcv'), may hold values from 0 to 31
- active: int32 [32, 32], P('src', 'rcv'), may hold values 0 or 1
Outputs:
- stacked: float32 [1024, 1024, 128], P('src', 'rcv')
Inputs may be any that keep to these rules, and one draw needn't show every extreme that they name: src_owner names a slot of the rcv dimension. rcv_owner names a slot of the src dimension.
All inputs are finite; a program needn't handle non-finite values. No bound on the sum of `active` on one device may be relied on, other than what follows from the above.
Results may differ from a plain program's by a relative error of at most 0.004.
Values may be sent and summed in bfloat16 or wider, within the bound.
A program may use at most 128 MiB of HBM per device.

v0:
```python
import jax
import jax.numpy as jnp
from jax import lax
from jax.experimental import pallas as pl
from jax.experimental.pallas import tpu as pltpu
from jax.sharding import PartitionSpec as P

LAGS = 128
BLOCK = 32
FINE = 16

epsilon = 1e-06


def from_root(value, axis, source):
    kept = jnp.where(lax.axis_index(axis) == source, value, 0).astype(value.dtype)
    return lax.psum(kept, axis)


def normalise(traces):
    values = traces.astype(jnp.float32)
    energy = jnp.mean(values * values, axis=-1, keepdims=True)
    return (values * lax.rsqrt(energy + epsilon)).astype(jnp.bfloat16)


def correlate_kernel(active_ref, a_ref, bt_ref, out_hbm, toep, lagged, out_v, sem):
    wins, src, samples = a_ref.shape
    scale = 1.0 / (float((samples - LAGS) * wins) ** 0.5)
    lane = lax.broadcasted_iota(jnp.int32, (src, samples), 1)
    for w in range(wins):
        a = jnp.where(lane < samples - LAGS, a_ref[w].astype(jnp.float32), 0.0)
        for k in range(FINE):
            rolled = a if k == 0 else pltpu.roll(a, k, 1)
            toep[k * src : (k + 1) * src, w * samples : (w + 1) * samples] = rolled.astype(jnp.bfloat16)
    depth = wins * samples
    group = lax.broadcasted_iota(jnp.int32, (1, LAGS), 1) // BLOCK
    factor = jnp.zeros((1, LAGS), jnp.float32)
    for g in range(LAGS // BLOCK):
        factor = jnp.where(group == g, active_ref[0, g].astype(jnp.float32) * scale, factor)

    def step(pair, carry):
        base = pl.multiple_of(pair * 2 * FINE, FINE)
        both = jnp.concatenate([bt_ref[pl.ds(base, depth), :], bt_ref[pl.ds(base + FINE, depth), :]], axis=1)
        acc = jnp.dot(toep[...], both, preferred_element_type=jnp.float32)
        for jj in range(2):
            for k in range(FINE):
                lagged[pl.ds(base + FINE * jj + k, src, stride=LAGS), :] = (
                    acc[k * src : (k + 1) * src, jj * 128 : (jj + 1) * 128] * factor
                )
        return carry

    lax.fori_loop(0, LAGS // FINE // 2, step, 0)
    for s in range(src):
        out_v[s] = lagged[s * LAGS : (s + 1) * LAGS, :].T
        if s % 8 == 7:
            part = pl.ds(s - 7, 8)
            pltpu.make_async_copy(out_v.at[part], out_hbm.at[part], sem.at[s // 8]).start()
    for q in range(src // 8):
        part = pl.ds(q * 8, 8)
        pltpu.make_async_copy(out_v.at[part], out_hbm.at[part], sem.at[q]).wait()


def correlate(active, a, bt):
    wins, src, samples = a.shape
    rcv = bt.shape[1]
    return pl.pallas_call(
        correlate_kernel,
        out_shape=jax.ShapeDtypeStruct((src, rcv, LAGS), jnp.float32),
        in_specs=[
            pl.BlockSpec(memory_space=pltpu.SMEM),
            pl.BlockSpec(memory_space=pltpu.VMEM),
            pl.BlockSpec(memory_space=pltpu.VMEM),
        ],
        out_specs=pl.BlockSpec(memory_space=pl.ANY),
        scratch_shapes=[
            pltpu.VMEM((FINE * src, wins * samples), jnp.bfloat16),
            pltpu.VMEM((src * LAGS, rcv), jnp.float32),
            pltpu.VMEM((src, rcv, LAGS), jnp.float32),
            pltpu.SemaphoreType.DMA((src // 8,)),
        ],
        compiler_params=pltpu.CompilerParams(vmem_limit_bytes=48 * 2**20),
    )(active, a, bt)


def body(src_traces, rcv_traces, src_owner, rcv_owner, active):
    sources = normalise(src_traces[:, 0])
    receivers = normalise(rcv_traces[:, 0])
    wins, rcv, samples = receivers.shape
    source_rows = from_root(sources, "rcv", src_owner[:, :, None])
    receiver_rows = from_root(receivers, "src", rcv_owner[:, :, None])
    late = jnp.transpose(receiver_rows, (0, 2, 1)).reshape(wins * samples, rcv)
    late = jnp.concatenate([late, jnp.zeros((LAGS, rcv), jnp.bfloat16)], axis=0)
    return correlate(active, source_rows, late)


def solution(mesh):
    return jax.shard_map(
        body,
        mesh=mesh,
        in_specs=(
            P(None, "rcv", "src", None),
            P(None, "src", "rcv", None),
            P(None, "src"),
            P(None, "rcv"),
            P("src", "rcv"),
        ),
        out_specs=P("src", "rcv", None),
        check_vma=False,
    )
```

profile of v0, /device:TPU:6, one launch (start us, length us, event | category | flops | bytes accessed | tf_op | source)
XLA Modules:
  0.0 244.2 jit_solution(7842620159322720950)
XLA Ops:
  6.5 0.0 all-reduce.6.cloned.1.call-start
  6.5 1.5 fusion
  8.1 0.7 compare_bitcast_fusion
  8.7 2.1 fusion.3
  10.8 0.0 copy-start.2
  10.8 0.0 copy-start.3
  10.8 1.3 copy.7
  12.1 0.0 copy-start.1
  12.1 0.0 all-reduce.6.cloned.1.call-update
  12.2 0.0 all-reduce.4.cloned.1.call-start
  12.2 0.0 copy-done.2
  12.2 0.1 fusion.4
  12.3 0.0 copy-done.3
  12.4 0.9 fusion.6
  13.3 0.0 all-reduce.4.cloned.1.call-update
  13.3 151.4 %all-reduce.6.cloned.1.call-done = bf16[4096,128]{1,0:T(8,128)(2,1)} async-done(((bf16[4096,128]{1,0:T(8,128)(2,1)}), bf16[4096,128]{1,0:T(8,128)(2,1)}) %all-reduce.6.cloned.1.call-update) | async-done | bytes 1048592 | tf_op jit(solution)/shard_map/psum | solution.py:17
  164.7 1.3 concatenate.3.bt_ref
  166.0 61.0 %all-reduce.4.cloned.1.call-done.a_ref = bf16[2,32,2048]{2,1,0:T(8,128)(2,1)} async-done(((bf16[2,32,2048]{2,1,0:T(8,128)(2,1)}), bf16[2,32,2048]{2,1,0:T(8,128)(2,1)}) %all-reduce.4.cloned.1.call-update) | async-done | bytes 262160 | tf_op jit(solution)/shard_map/psum | solution.py:17
  227.1 0.0 copy-done.1
  227.1 0.0 copy-start
  227.1 0.9 copy-done
  228.0 9.3 %shard_map.55 = f32[32,128,128]{2,1,0:T(8,128)} custom-call(s32[1,4]{1,0:T(1,128)S(1)} %copy-done.1, bf16[2,32,2048]{2,1,0:T(8,128)(2,1)S(1)} %copy-done, bf16[4224,128]{1,0:T(8,128)(2,1)S(1)} %concatenate.3.bt_ref), custom_call_target="tpu_custom_call" | custom-call | tf_op jit(solution)/shard_map/pallas_call | solution.py:66
  (3 shorter events, 0.0 us)
Async XLA Ops:
  6.5 158.2 %all-reduce.6.cloned.1.call-start = ((), (), s32[]{:S(2)}) async-start(), calls=%async_computation.1 | async-start | bytes 2097152 | tf_op jit(solution)/shard_map/psum | solution.py:17
  10.8 1.4 copy-start.2
  10.8 1.5 copy-start.3
  12.1 214.9 %copy-start.1 = (s32[1,4]{1,0:T(1,128)S(1)}, s32[1,4]{1,0:T(1,128)}, u32[]{:S(2)}) copy-start(s32[1,4]{1,0:T(1,128)} %active_ref.1) | copy-start | bytes 52
  12.2 214.9 %all-reduce.4.cloned.1.call-start = ((), (), s32[]{:S(2)}) async-start(), calls=%async_computation | async-start | bytes 524288 | tf_op jit(solution)/shard_map/psum | solution.py:17
  227.1 1.0 copy-start
Sparse Core Ops, SparseCore 0:
  12.3 152.4 all-reduce.5
  167.0 59.9 all-reduce.3
where the time goes:
time: 247 us; the launch traced here: 244 us
  waiting for transfers between devices  213 us (86%)
  between operations  13.5 us (5%)
  Pallas kernels  9.27 us (4%)
  other arithmetic  5.27 us (2%)
  local copies, waits for them, and re-layouts  3.57 us (1%)
    psum x2, waiting for transfers between devices, from_root(): return lax.psum(kept, axis)  212 us
    pallas_call x1, Pallas kernels, correlate(): pl.pallas_call(correlate_kernel, out_shape=jax.ShapeDtypeStruct((src, rcv...  9.27 us
  transfers between devices with their start and end apart: 2, of which 2 were waited for; matrix products, arithmetic and copies ran while one was open for 1% of the time, Pallas kernels for 0%

commit v1 on v0

--- a/solution.py
+++ b/solution.py
@@ -1,34 +1,227 @@
 import jax
 import jax.numpy as jnp
+import numpy as np
 from jax import lax
 from jax.experimental import pallas as pl
 from jax.experimental.pallas import tpu as pltpu
 from jax.sharding import PartitionSpec as P
 
+MESH = pl.DeviceIdType.MESH
 LAGS = 128
 BLOCK = 32
 FINE = 16
+DEPTH_Z, DEPTH_Y = 8, 4
+
+HOPS = ((0, 1), (0, 1), (1, 1), (2, 0), (0, -1), (0, -1), (-1, -1), (-2, 0))
+STREAMS = len(HOPS)
+CHUNKS = 8
+STEPS = 4
+SLACK = 5
+ROUNDS = CHUNKS + (STEPS - 1) * SLACK
+ROUTES = (
+    (0, 0, 0, 0, 0, 0, 0, 0, 0, 0, 0, 0, 0, 0, 0, 0, 0, 0, 0, 0, 0, 0, 0, 0),
+    (0, 1, 0, 1, 0, 0, 1, 0, 0, 1, 2, 6, 7, 3, 5, 4, 1, 1, 4, 4, 4, 4, 4, 4),
+    (6, 1, 0, 1, 2, 3, 0, 1, 0, 1, 7, 6, 4, 5, 3, 2, 2, 2, 3, 3, 2, 2, 3, 3),
+    (0, 0, 4, 5, 4, 5, 5, 4, 7, 1, 6, 0, 4, 5, 2, 3, 4, 3, 3, 4, 1, 1, 3, 3),
+    (2, 0, 2, 2, 2, 3, 4, 0, 1, 3, 4, 6, 2, 7, 0, 5, 4, 3, 2, 3, 2, 4, 3, 4),
+    (3, 2, 2, 2, 2, 3, 0, 2, 4, 6, 2, 7, 0, 5, 1, 3, 3, 4, 1, 3, 3, 4, 4, 3),
+    (6, 1, 2, 2, 2, 6, 5, 2, 2, 7, 1, 5, 4, 6, 3, 0, 2, 4, 2, 3, 4, 3, 3, 4),
+    (3, 2, 3, 2, 4, 6, 6, 6, 2, 5, 1, 6, 4, 0, 3, 7, 3, 4, 3, 2, 3, 4, 2, 4),
+    (2, 3, 3, 3, 2, 7, 3, 0, 1, 4, 6, 3, 5, 0, 2, 7, 4, 3, 3, 1, 4, 3, 3, 3),
+    (2, 1, 3, 3, 3, 2, 1, 2, 6, 3, 4, 1, 2, 5, 0, 7, 4, 2, 3, 2, 3, 4, 4, 4),
+    (1, 3, 2, 2, 2, 5, 3, 2, 4, 3, 2, 1, 0, 5, 7, 6, 4, 3, 2, 3, 4, 3, 4, 4),
+    (3, 2, 3, 3, 2, 3, 3, 2, 2, 1, 6, 0, 7, 3, 4, 5, 3, 4, 4, 4, 4, 2, 4, 4),
+    (3, 2, 3, 3, 2, 3, 4, 2, 6, 7, 4, 5, 3, 2, 0, 1, 4, 4, 3, 3, 3, 3, 4, 4),
+    (3, 2, 2, 3, 3, 2, 3, 2, 5, 4, 3, 2, 0, 1, 7, 6, 4, 4, 2, 2, 4, 4, 4, 4),
+    (1, 2, 3, 3, 2, 3, 3, 2, 3, 2, 0, 1, 7, 6, 5, 4, 3, 3, 3, 3, 4, 4, 4, 4),
+    (7, 6, 7, 2, 6, 7, 6, 6, 3, 1, 2, 0, 5, 4, 7, 6, 4, 4, 3, 4, 4, 4, 3, 3),
+    (3, 7, 3, 3, 7, 3, 7, 7, 4, 5, 6, 3, 1, 0, 2, 7, 4, 4, 4, 2, 4, 4, 4, 2),
+    (3, 7, 3, 0, 7, 3, 7, 1, 7, 3, 5, 0, 2, 6, 4, 1, 3, 3, 4, 3, 4, 4, 4, 3),
+    (3, 7, 2, 3, 7, 3, 6, 7, 1, 0, 3, 2, 5, 4, 7, 6, 4, 4, 3, 3, 4, 4, 3, 3),
+    (3, 7, 3, 5, 3, 7, 3, 7, 2, 6, 0, 5, 7, 3, 1, 4, 4, 4, 4, 3, 3, 3, 4, 3),
+    (0, 7, 7, 6, 7, 6, 7, 7, 6, 7, 4, 5, 3, 2, 1, 0, 3, 3, 4, 4, 4, 4, 3, 3),
+    (2, 3, 2, 2, 3, 2, 3, 6, 7, 1, 3, 2, 5, 4, 6, 0, 4, 4, 3, 3, 4, 4, 3, 4),
+    (6, 7, 7, 6, 7, 6, 7, 6, 3, 2, 1, 0, 6, 7, 4, 5, 4, 4, 4, 4, 3, 3, 3, 3),
+    (6, 7, 7, 6, 7, 6, 6, 7, 5, 4, 3, 2, 0, 1, 7, 6, 4, 4, 4, 4, 4, 4, 2, 2),
+    (7, 6, 7, 0, 7, 6, 7, 7, 4, 0, 6, 3, 1, 5, 2, 7, 3, 4, 3, 3, 3, 4, 3, 1),
+    (6, 7, 0, 6, 7, 6, 7, 7, 7, 2, 1, 3, 5, 6, 4, 0, 2, 4, 4, 4, 4, 3, 3, 2),
+    (6, 1, 4, 6, 6, 4, 6, 6, 1, 7, 3, 2, 4, 0, 6, 5, 3, 3, 4, 4, 3, 4, 2, 3),
+    (6, 7, 7, 4, 7, 4, 7, 7, 1, 6, 5, 3, 7, 2, 0, 4, 4, 3, 4, 4, 2, 4, 3, 2),
+    (2, 6, 5, 6, 5, 6, 6, 6, 3, 6, 5, 1, 2, 0, 7, 4, 4, 2, 3, 4, 3, 4, 4, 3),
+    (1, 7, 2, 2, 2, 7, 7, 6, 6, 1, 7, 3, 0, 5, 4, 2, 3, 3, 2, 4, 4, 3, 3, 2),
+    (6, 7, 4, 4, 4, 6, 6, 6, 7, 0, 1, 5, 3, 6, 4, 2, 3, 4, 3, 4, 4, 2, 2, 3),
+    (0, 7, 0, 6, 6, 7, 6, 6, 1, 5, 4, 7, 2, 0, 6, 3, 4, 3, 4, 3, 4, 3, 1, 3),
+)
 
 epsilon = 1e-06
 
 
-def from_root(value, axis, source):
-    kept = jnp.where(lax.axis_index(axis) == source, value, 0).astype(value.dtype)
-    return lax.psum(kept, axis)
-
-
-def normalise(traces):
-    values = traces.astype(jnp.float32)
+def normalised(values):
     energy = jnp.mean(values * values, axis=-1, keepdims=True)
-    return (values * lax.rsqrt(energy + epsilon)).astype(jnp.bfloat16)
+    return values * lax.rsqrt(energy + epsilon)
+
+
+def spread_kernel(routes, src_owner, rcv_owner, src_ref, rcv_ref, a_out, bt_out, a_own, a_cand, a_all, own, *rest):
+    wins = rcv_ref.shape[0]
+    samples = rcv_ref.shape[-1]
+    held = [rest[w * ROUNDS : (w + 1) * ROUNDS] for w in range(wins)]
+    sent = [rest[(wins + w) * ROUNDS : (wins + w + 1) * ROUNDS] for w in range(wins)]
+    send_sem, recv_sem, a_send, a_recv = rest[2 * wins * ROUNDS :]
+    place = lax.axis_index("src")
+    me = lax.axis_index("rcv")
+    z, y = place // DEPTH_Y, place % DEPTH_Y
+    others = a_own.shape[0] - 1
+
+    def partner(i):
+        dz, dy = HOPS[i]
+        return {"src": lax.rem(z + dz + DEPTH_Z, DEPTH_Z) * DEPTH_Y + lax.rem(y + dy + DEPTH_Y, DEPTH_Y)}
+
+    def peer(i):
+        return lax.rem(me + 1 + i, others + 1)
+
+    barrier = pltpu.get_barrier_semaphore()
+    seen = []
+    for i in range(STREAMS):
+        if HOPS[i] not in seen:
+            seen.append(HOPS[i])
+            pl.semaphore_signal(barrier, inc=1, device_id=partner(i), device_id_type=MESH)
+    for i in range(others):
+        pl.semaphore_signal(barrier, inc=1, device_id={"rcv": peer(i)}, device_id_type=MESH)
+
+    width = samples // (others + 1)
+    for w in range(wins):
+        rows = normalised(src_ref[w, 0].astype(jnp.float32)).astype(jnp.bfloat16)
+        for i in range(others + 1):
+            a_own[i, w] = rows[:, i * width : (i + 1) * width]
+        rows = normalised(rcv_ref[w, 0].astype(jnp.float32))
+        for t in range(samples // LAGS):
+            own[pl.ds(w * samples + t * LAGS, LAGS), :] = rows[:, t * LAGS : (t + 1) * LAGS].T.astype(jnp.bfloat16)
+    pl.semaphore_wait(barrier, len(seen) + others)
+
+    piece = samples // (CHUNKS * STREAMS)
+
+    def rows_of(w, c, j):
+        return pl.ds(w * samples + (c * STREAMS + j) * piece, piece)
+
+    root, row = [], []
+    for w in range(wins):
+        far = rcv_owner[w, 0]
+        root.append(far == place)
+        dz = lax.rem(z - far // DEPTH_Y + DEPTH_Z, DEPTH_Z)
+        dy = lax.rem(y - far % DEPTH_Y + DEPTH_Y, DEPTH_Y)
+        row.append((dz * DEPTH_Y + dy) * (3 * STREAMS))
+
+    def arrived(w, r):
+        pltpu.make_async_copy(held[w][r], held[w][r], recv_sem.at[w, r]).wait()
+
+    def a_wait(sem, k, ref):
+        pltpu.make_async_copy(ref.at[pl.ds(0, others)], ref.at[pl.ds(0, others)], sem.at[k]).wait()
+
+    for i in range(others):
+        pltpu.make_async_remote_copy(
+            src_ref=a_own.at[peer(i)],
+            dst_ref=a_cand.at[me],
+            send_sem=a_send.at[0],
+            recv_sem=a_recv.at[0],
+            device_id={"rcv": peer(i)},
+            device_id_type=MESH,
+        ).start()
+
+    def a_pass():
+        a_wait(a_recv, 0, a_cand)
+        for w in range(wins):
+            who = src_owner[w, 0]
+            a_all[me, w] = jnp.where(who == me, a_own[me, w], a_cand[who, w])
+        for i in range(others):
+            pltpu.make_async_remote_copy(
+                src_ref=a_all.at[me],
+                dst_ref=a_all.at[me],
+                send_sem=a_send.at[1],
+                recv_sem=a_recv.at[1],
+                device_id={"rcv": peer(i)},
+                device_id_type=MESH,
+            ).start()
+
+    forward = [[routes[row[w] + i] for i in range(STREAMS)] for w in range(wins)]
+    for r in range(ROUNDS):
+        for w in range(wins):
+            if r >= SLACK:
+                arrived(w, r - SLACK)
+                for i in range(STREAMS):
+                    value = held[w][r - SLACK][forward[w][i]]
+                    if r < CHUNKS:
+                        value = jnp.where(root[w], own[rows_of(w, r, i), :], value)
+                    sent[w][r][i] = value
+            for i in range(STREAMS):
+                pltpu.make_async_remote_copy(
+                    src_ref=sent[w][r].at[i] if r >= SLACK else own.at[rows_of(w, min(r, CHUNKS - 1), i), :],
+                    dst_ref=held[w][r].at[i],
+                    send_sem=send_sem.at[w, r],
+                    recv_sem=recv_sem.at[w, r],
+                    device_id=partner(i),
+                    device_id_type=MESH,
+                ).start()
+        if r == SLACK:
+            a_pass()
+    for r in range(max(0, ROUNDS - SLACK), ROUNDS):
+        for w in range(wins):
+            arrived(w, r)
+
+    for w in range(wins):
+        slot = [routes[row[w] + STREAMS + j] for j in range(STREAMS)]
+        step = [routes[row[w] + 2 * STREAMS + j] for j in range(STREAMS)]
+        for c in range(CHUNKS):
+            for j in range(STREAMS):
+                value = own[rows_of(w, c, j), :]
+                for d in range(1, STEPS + 1):
+                    value = jnp.where(step[j] == d, held[w][c + (d - 1) * SLACK][slot[j]], value)
+                bt_out[rows_of(w, c, j), :] = value
+    bt_out[pl.ds(wins * samples, LAGS), :] = jnp.zeros((LAGS, bt_out.shape[1]), jnp.bfloat16)
+    a_wait(a_recv, 1, a_all)
+    a_out[...] = a_all[...]
+
+    a_wait(a_send, 0, a_all)
+    a_wait(a_send, 1, a_all)
+    for r in range(ROUNDS):
+        for w in range(wins):
+            pltpu.make_async_copy(held[w][r], held[w][r], send_sem.at[w, r]).wait()
+
+
+def spread(src_owner, rcv_owner, src_traces, rcv_traces, peers):
+    wins, _, src, samples = src_traces.shape
+    rcv = rcv_traces.shape[2]
+    routes = jnp.asarray(np.array(ROUTES, np.int32).reshape(-1))
+    piece = samples // (CHUNKS * STREAMS)
+    parts = pltpu.VMEM((peers, wins, src, samples // peers), jnp.bfloat16)
+    smem, vmem = pl.BlockSpec(memory_space=pltpu.SMEM), pl.BlockSpec(memory_space=pltpu.VMEM)
+    return pl.pallas_call(
+        spread_kernel,
+        out_shape=(
+            jax.ShapeDtypeStruct((peers, wins, src, samples // peers), jnp.bfloat16),
+            jax.ShapeDtypeStruct((wins * samples + LAGS, rcv), jnp.bfloat16),
+        ),
+        in_specs=[smem, smem, smem, vmem, vmem],
+        out_specs=(vmem, vmem),
+        scratch_shapes=[parts, parts, parts, pltpu.VMEM((wins * samples, rcv), jnp.bfloat16)]
+        + [pltpu.VMEM((STREAMS, piece, rcv), jnp.bfloat16)] * (2 * wins * ROUNDS)
+        + [
+            pltpu.SemaphoreType.DMA((wins, ROUNDS)),
+            pltpu.SemaphoreType.DMA((wins, ROUNDS)),
+            pltpu.SemaphoreType.DMA((2,)),
+            pltpu.SemaphoreType.DMA((2,)),
+        ],
+        compiler_params=pltpu.CompilerParams(collective_id=0, has_side_effects=True, vmem_limit_bytes=40 * 2**20),
+    )(routes, src_owner, rcv_owner, src_traces, rcv_traces)
 
 
 def correlate_kernel(active_ref, a_ref, bt_ref, out_hbm, toep, lagged, out_v, sem):
-    wins, src, samples = a_ref.shape
+    parts, wins, src, width = a_ref.shape
+    samples = parts * width
     scale = 1.0 / (float((samples - LAGS) * wins) ** 0.5)
     lane = lax.broadcasted_iota(jnp.int32, (src, samples), 1)
     for w in range(wins):
-        a = jnp.where(lane < samples - LAGS, a_ref[w].astype(jnp.float32), 0.0)
+        a = jnp.concatenate([a_ref[i, w] for i in range(parts)], axis=1).astype(jnp.float32)
+        a = jnp.where(lane < samples - LAGS, a, 0.0)
         for k in range(FINE):
             rolled = a if k == 0 else pltpu.roll(a, k, 1)
             toep[k * src : (k + 1) * src, w * samples : (w + 1) * samples] = rolled.astype(jnp.bfloat16)
@@ -61,7 +254,7 @@
 
 
 def correlate(active, a, bt):
-    wins, src, samples = a.shape
+    parts, wins, src, width = a.shape
     rcv = bt.shape[1]
     return pl.pallas_call(
         correlate_kernel,
@@ -73,27 +266,22 @@
         ],
         out_specs=pl.BlockSpec(memory_space=pl.ANY),
         scratch_shapes=[
-            pltpu.VMEM((FINE * src, wins * samples), jnp.bfloat16),
+            pltpu.VMEM((FINE * src, parts * width * wins), jnp.bfloat16),
             pltpu.VMEM((src * LAGS, rcv), jnp.float32),
             pltpu.VMEM((src, rcv, LAGS), jnp.float32),
             pltpu.SemaphoreType.DMA((src // 8,)),
         ],
-        compiler_params=pltpu.CompilerParams(vmem_limit_bytes=48 * 2**20),
+        compiler_params=pltpu.CompilerParams(vmem_limit_bytes=40 * 2**20),
     )(active, a, bt)
 
 
-def body(src_traces, rcv_traces, src_owner, rcv_owner, active):
-    sources = normalise(src_traces[:, 0])
-    receivers = normalise(rcv_traces[:, 0])
-    wins, rcv, samples = receivers.shape
-    source_rows = from_root(sources, "rcv", src_owner[:, :, None])
-    receiver_rows = from_root(receivers, "src", rcv_owner[:, :, None])
-    late = jnp.transpose(receiver_rows, (0, 2, 1)).reshape(wins * samples, rcv)
-    late = jnp.concatenate([late, jnp.zeros((LAGS, rcv), jnp.bfloat16)], axis=0)
-    return correlate(active, source_rows, late)
-
-
 def solution(mesh):
+    peers = mesh.shape["rcv"]
+
+    def body(src_traces, rcv_traces, src_owner, rcv_owner, active):
+        a, bt = spread(src_owner, rcv_owner, src_traces, rcv_traces, peers)
+        return correlate(active, a, bt)
+
     return jax.shard_map(
         body,
         mesh=mesh,

time: 247 us -> 53.2 us (0.22)
  the two profiles are of different devices: /device:TPU:6 before, /device:TPU:1 now
where the time goes in v1:
time: 53.2 us; the launch traced here: 53 us
  Pallas kernels  48 us (90%)
  local copies, waits for them, and re-layouts  4.99 us (9%)
    pallas_call x1, Pallas kernels, spread(): pl.pallas_call(spread_kernel, out_shape=(jax.ShapeDtypeStruct((peers, win...  38.7 us
    pallas_call x1, Pallas kernels, correlate(): pl.pallas_call(correlate_kernel, out_shape=jax.ShapeDtypeStruct((src, rcv...  9.28 us
    unnamed x10, local copies, waits for them, and re-layouts  4.99 us

profile of v1, /device:TPU:1, one launch (start us, length us, event | category | flops | bytes accessed | tf_op | source)
XLA Modules:
  0.0 53.0 jit_solution(1707370270105900935)
XLA Ops:
  0.0 0.7 %copy.7.src_owner = s32[2,1]{1,0:T(2,128)S(1)} copy(s32[2,1]{0,1:T(1,128)} %param.8) | data formatting | bytes 16 | tf_op args[2]
  0.7 0.7 %copy.8.rcv_owner = s32[2,1]{1,0:T(2,128)S(1)} copy(s32[2,1]{0,1:T(1,128)} %param.9) | data formatting | bytes 16 | tf_op args[3]
  1.5 0.0 copy-start
  1.5 1.2 %copy-done = bf16[2,1,128,2048]{3,2,1,0:T(8,128)(2,1)S(1)} copy-done((bf16[2,1,128,2048]{3,2,1,0:T(8,128)(2,1)S(1)}, bf16[2,1,128,2048]{3,2,1,0:T(8,128)(2,1)}, u32[]{:S(2)}) %copy-start) | copy-done | bytes 1048600
  2.7 0.0 copy-start.1
  2.7 0.9 %copy-done.1 = bf16[2,1,32,2048]{3,2,1,0:T(8,128)(2,1)S(1)} copy-done((bf16[2,1,32,2048]{3,2,1,0:T(8,128)(2,1)S(1)}, bf16[2,1,32,2048]{3,2,1,0:T(8,128)(2,1)}, u32[]{:S(2)}) %copy-start.1) | copy-done | bytes 262168
  3.7 0.0 copy-start.2
  3.7 0.7 %copy-done.2 = s32[768]{0:T(1024)S(1)} copy-done((s32[768]{0:T(1024)S(1)}, s32[768]{0:T(1024)}, u32[]{:S(2)}) %copy-start.2) | copy-done | bytes 3096
  4.3 38.7 %shard_map.64 = (bf16[8,2,32,256]{3,2,1,0:T(8,128)(2,1)S(1)}, bf16[4224,128]{1,0:T(8,128)(2,1)S(1)}) custom-call(s32[768]{0:T(1024)S(1)} %copy-done.2, s32[2,1]{1,0:T(2,128)S(1)} %copy.7.src_owner, s32[2,1]{1,0:T(2,128)S(1)} %copy.8.rcv_owner, bf16[2,1,32,2048]{3,2,1,0:T(8,128)(2,1)S(1)} %copy-done.1, bf16[2,1,128,2048]{3,2,1,0:T(8,128)(2,1)S(1)} %copy-done), custom_call_target="tpu_custom_call" | custom-call | tf_op jit(solution)/shard_map/pallas_call | solution.py:197
  43.0 0.0 copy-start.3
  43.1 0.6 %copy-done.3 = s32[1,4]{1,0:T(1,128)S(1)} copy-done((s32[1,4]{1,0:T(1,128)S(1)}, s32[1,4]{1,0:T(1,128)}, u32[]{:S(2)}) %copy-start.3) | copy-done | bytes 40
  43.7 9.3 %shard_map.65 = f32[32,128,128]{2,1,0:T(8,128)} custom-call(s32[1,4]{1,0:T(1,128)S(1)} %copy-done.3, bf16[8,2,32,256]{3,2,1,0:T(8,128)(2,1)S(1)} %get-tuple-element.7.a_ref, bf16[4224,128]{1,0:T(8,128)(2,1)S(1)} %get-tuple-element.8.bt_ref), custom_call_target="tpu_custom_call" | custom-call | tf_op jit(solution)/shard_map/pallas_call | solution.py:259
Async XLA Ops:
  1.5 1.2 %copy-start = (bf16[2,1,128,2048]{3,2,1,0:T(8,128)(2,1)S(1)}, bf16[2,1,128,2048]{3,2,1,0:T(8,128)(2,1)}, u32[]{:S(2)}) copy-start(bf16[2,1,128,2048]{3,2,1,0:T(8,128)(2,1)} %rcv_ref.1) | copy-start | bytes 3145732
  2.7 0.9 %copy-start.1 = (bf16[2,1,32,2048]{3,2,1,0:T(8,128)(2,1)S(1)}, bf16[2,1,32,2048]{3,2,1,0:T(8,128)(2,1)}, u32[]{:S(2)}) copy-start(bf16[2,1,32,2048]{3,2,1,0:T(8,128)(2,1)} %src_ref.1) | copy-start | bytes 786436
  3.7 0.7 %copy-start.2 = (s32[768]{0:T(1024)S(1)}, s32[768]{0:T(1024)}, u32[]{:S(2)}) copy-start(s32[768]{0:T(1024)} %constant.2.clone.routes) | copy-start | bytes 9220
  43.0 0.7 %copy-start.3 = (s32[1,4]{1,0:T(1,128)S(1)}, s32[1,4]{1,0:T(1,128)}, u32[]{:S(2)}) copy-start(s32[1,4]{1,0:T(1,128)} %active_ref.1) | copy-start | bytes 52

commit v2 on v1

v2 whole, which is shorter than its diff:
```python
import jax
import jax.numpy as jnp
import numpy as np
from jax import lax
from jax.experimental import pallas as pl
from jax.experimental.pallas import tpu as pltpu
from jax.sharding import PartitionSpec as P

MESH = pl.DeviceIdType.MESH
LAGS = 128
BLOCK = 32
FINE = 16
DEPTH_Z, DEPTH_Y = 8, 4

HOPS = ((0, 1), (0, 1), (1, 1), (2, 0), (0, -1), (0, -1), (-1, -1), (-2, 0))
STREAMS = len(HOPS)
CHUNKS = 8
STEPS = 4
SLACK = 4
A_GATHER = 4
A_ROLL = 12
PASSES = (4, 6, 8)
ROUNDS = CHUNKS + (STEPS - 1) * SLACK
ROUTES = (
    (0, 0, 0, 0, 0, 0, 0, 0, 0, 0, 0, 0, 0, 0, 0, 0, 0, 0, 0, 0, 0, 0, 0, 0),
    (0, 1, 0, 1, 0, 0, 1, 0, 0, 1, 2, 6, 7, 3, 5, 4, 1, 1, 4, 4, 4, 4, 4, 4),
    (6, 1, 0, 1, 2, 3, 0, 1, 0, 1, 7, 6, 4, 5, 3, 2, 2, 2, 3, 3, 2, 2, 3, 3),
    (0, 0, 4, 5, 4, 5, 5, 4, 7, 1, 6, 0, 4, 5, 2, 3, 4, 3, 3, 4, 1, 1, 3, 3),
    (2, 0, 2, 2, 2, 3, 4, 0, 1, 3, 4, 6, 2, 7, 0, 5, 4, 3, 2, 3, 2, 4, 3, 4),
    (3, 2, 2, 2, 2, 3, 0, 2, 4, 6, 2, 7, 0, 5, 1, 3, 3, 4, 1, 3, 3, 4, 4, 3),
    (6, 1, 2, 2, 2, 6, 5, 2, 2, 7, 1, 5, 4, 6, 3, 0, 2, 4, 2, 3, 4, 3, 3, 4),
    (3, 2, 3, 2, 4, 6, 6, 6, 2, 5, 1, 6, 4, 0, 3, 7, 3, 4, 3, 2, 3, 4, 2, 4),
    (2, 3, 3, 3, 2, 7, 3, 0, 1, 4, 6, 3, 5, 0, 2, 7, 4, 3, 3, 1, 4, 3, 3, 3),
    (2, 1, 3, 3, 3, 2, 1, 2, 6, 3, 4, 1, 2, 5, 0, 7, 4, 2, 3, 2, 3, 4, 4, 4),
    (1, 3, 2, 2, 2, 5, 3, 2, 4, 3, 2, 1, 0, 5, 7, 6, 4, 3, 2, 3, 4, 3, 4, 4),
    (3, 2, 3, 3, 2, 3, 3, 2, 2, 1, 6, 0, 7, 3, 4, 5, 3, 4, 4, 4, 4, 2, 4, 4),
    (3, 2, 3, 3, 2, 3, 4, 2, 6, 7, 4, 5, 3, 2, 0, 1, 4, 4, 3, 3, 3, 3, 4, 4),
    (3, 2, 2, 3, 3, 2, 3, 2, 5, 4, 3, 2, 0, 1, 7, 6, 4, 4, 2, 2, 4, 4, 4, 4),
    (1, 2, 3, 3, 2, 3, 3, 2, 3, 2, 0, 1, 7, 6, 5, 4, 3, 3, 3, 3, 4, 4, 4, 4),
    (7, 6, 7, 2, 6, 7, 6, 6, 3, 1, 2, 0, 5, 4, 7, 6, 4, 4, 3, 4, 4, 4, 3, 3),
    (3, 7, 3, 3, 7, 3, 7, 7, 4, 5, 6, 3, 1, 0, 2, 7, 4, 4, 4, 2, 4, 4, 4, 2),
    (3, 7, 3, 0, 7, 3, 7, 1, 7, 3, 5, 0, 2, 6, 4, 1, 3, 3, 4, 3, 4, 4, 4, 3),
    (3, 7, 2, 3, 7, 3, 6, 7, 1, 0, 3, 2, 5, 4, 7, 6, 4, 4, 3, 3, 4, 4, 3, 3),
    (3, 7, 3, 5, 3, 7, 3, 7, 2, 6, 0, 5, 7, 3, 1, 4, 4, 4, 4, 3, 3, 3, 4, 3),
    (0, 7, 7, 6, 7, 6, 7, 7, 6, 7, 4, 5, 3, 2, 1, 0, 3, 3, 4, 4, 4, 4, 3, 3),
    (2, 3, 2, 2, 3, 2, 3, 6, 7, 1, 3, 2, 5, 4, 6, 0, 4, 4, 3, 3, 4, 4, 3, 4),
    (6, 7, 7, 6, 7, 6, 7, 6, 3, 2, 1, 0, 6, 7, 4, 5, 4, 4, 4, 4, 3, 3, 3, 3),
    (6, 7, 7, 6, 7, 6, 6, 7, 5, 4, 3, 2, 0, 1, 7, 6, 4, 4, 4, 4, 4, 4, 2, 2),
    (7, 6, 7, 0, 7, 6, 7, 7, 4, 0, 6, 3, 1, 5, 2, 7, 3, 4, 3, 3, 3, 4, 3, 1),
    (6, 7, 0, 6, 7, 6, 7, 7, 7, 2, 1, 3, 5, 6, 4, 0, 2, 4, 4, 4, 4, 3, 3, 2),
    (6, 1, 4, 6, 6, 4, 6, 6, 1, 7, 3, 2, 4, 0, 6, 5, 3, 3, 4, 4, 3, 4, 2, 3),
    (6, 7, 7, 4, 7, 4, 7, 7, 1, 6, 5, 3, 7, 2, 0, 4, 4, 3, 4, 4, 2, 4, 3, 2),
    (2, 6, 5, 6, 5, 6, 6, 6, 3, 6, 5, 1, 2, 0, 7, 4, 4, 2, 3, 4, 3, 4, 4, 3),
    (1, 7, 2, 2, 2, 7, 7, 6, 6, 1, 7, 3, 0, 5, 4, 2, 3, 3, 2, 4, 4, 3, 3, 2),
    (6, 7, 4, 4, 4, 6, 6, 6, 7, 0, 1, 5, 3, 6, 4, 2, 3, 4, 3, 4, 4, 2, 2, 3),
    (0, 7, 0, 6, 6, 7, 6, 6, 1, 5, 4, 7, 2, 0, 6, 3, 4, 3, 4, 3, 4, 3, 1, 3),
)

epsilon = 1e-06


def normalised(values):
    energy = jnp.mean(values * values, axis=-1, keepdims=True)
    return values * lax.rsqrt(energy + epsilon)


def spread_kernel(
    routes_hbm, src_owner_hbm, rcv_owner_hbm, active_hbm, src_hbm, rcv_hbm,
    lagged,
    routes, src_owner, rcv_owner, active, src_ref, rcv_ref, a_own, a_cand, a_all, own, bt, toep, acc,
    load_sem, send_sem, recv_sem, a_send, a_recv,
    *rest,
):
    wins, _, rcv, samples = rcv_ref.shape
    src = src_ref.shape[2]
    held = [rest[w * ROUNDS : (w + 1) * ROUNDS] for w in range(wins)]
    sent = [rest[(wins + w) * ROUNDS : (wins + w + 1) * ROUNDS] for w in range(wins)]
    place = lax.axis_index("src")
    me = lax.axis_index("rcv")
    z, y = place // DEPTH_Y, place % DEPTH_Y
    others = a_own.shape[0] - 1

    def partner(i):
        dz, dy = HOPS[i]
        return {"src": lax.rem(z + dz + DEPTH_Z, DEPTH_Z) * DEPTH_Y + lax.rem(y + dy + DEPTH_Y, DEPTH_Y)}

    def peer(i):
        return lax.rem(me + 1 + i, others + 1)

    barrier = pltpu.get_barrier_semaphore()
    seen = []
    for i in range(STREAMS):
        if HOPS[i] not in seen:
            seen.append(HOPS[i])
            pl.semaphore_signal(barrier, inc=1, device_id=partner(i), device_id_type=MESH)
    for i in range(others):
        pl.semaphore_signal(barrier, inc=1, device_id={"rcv": peer(i)}, device_id_type=MESH)

    loads = [pltpu.make_async_copy(rcv_hbm.at[w], rcv_ref.at[w], load_sem.at[w]) for w in range(wins)]
    small = ((src_hbm, src_ref), (routes_hbm, routes), (src_owner_hbm, src_owner), (rcv_owner_hbm, rcv_owner), (active_hbm, active))
    loads += [pltpu.make_async_copy(a, b, load_sem.at[wins + i]) for i, (a, b) in enumerate(small)]
    for load in loads:
        load.start()

    width = samples // (others + 1)
    for w in range(wins):
        loads[w].wait()
        rows = normalised(rcv_ref[w, 0].astype(jnp.float32))
        for t in range(samples // LAGS):
            own[pl.ds(w * samples + t * LAGS, LAGS), :] = rows[:, t * LAGS : (t + 1) * LAGS].T.astype(jnp.bfloat16)
    loads[wins].wait()
    for w in range(wins):
        rows = normalised(src_ref[w, 0].astype(jnp.float32)).astype(jnp.bfloat16)
        for i in range(others + 1):
            a_own[i, w] = rows[:, i * width : (i + 1) * width]
    for load in loads[wins + 1 :]:
        load.wait()
    pl.semaphore_wait(barrier, len(seen) + others)

    piece = samples // (CHUNKS * STREAMS)

    def rows_of(w, c, j):
        return pl.ds(w * samples + (c * STREAMS + j) * piece, piece)

    root, row = [], []
    for w in range(wins):
        far = rcv_owner[0, w]
        root.append(far == place)
        dz = lax.rem(z - far // DEPTH_Y + DEPTH_Z, DEPTH_Z)
        dy = lax.rem(y - far % DEPTH_Y + DEPTH_Y, DEPTH_Y)
        row.append((dz * DEPTH_Y + dy) * (3 * STREAMS))

    def arrived(w, r):
        pltpu.make_async_copy(held[w][r], held[w][r], recv_sem.at[w, r]).wait()

    def a_wait(sem, k, ref):
        pltpu.make_async_copy(ref.at[pl.ds(0, others)], ref.at[pl.ds(0, others)], sem.at[k]).wait()

    def a_scatter():
        for i in range(others):
            pltpu.make_async_remote_copy(
                src_ref=a_own.at[peer(i)],
                dst_ref=a_cand.at[me],
                send_sem=a_send.at[0],
                recv_sem=a_recv.at[0],
                device_id={"rcv": peer(i)},
                device_id_type=MESH,
            ).start()

    def a_gather():
        a_wait(a_recv, 0, a_cand)
        for w in range(wins):
            who = src_owner[0, w]
            a_all[me, w] = jnp.where(who == me, a_own[me, w], a_cand[who, w])
        for i in range(others):
            pltpu.make_async_remote_copy(
                src_ref=a_all.at[me],
                dst_ref=a_all.at[me],
                send_sem=a_send.at[1],
                recv_sem=a_recv.at[1],
                device_id={"rcv": peer(i)},
                device_id_type=MESH,
            ).start()

    lane = lax.broadcasted_iota(jnp.int32, (src, samples), 1)

    def roll_part(k):
        for w in range(wins):
            a = jnp.concatenate([a_all[i, w] for i in range(others + 1)], axis=1).astype(jnp.float32)
            a = jnp.where(lane < samples - LAGS, a, 0.0)
            rolled = a if k == 0 else pltpu.roll(a, k, 1)
            toep[pl.ds(k * src, src), w * samples : (w + 1) * samples] = rolled.astype(jnp.bfloat16)

    forward = [[routes[row[w] + i] for i in range(STREAMS)] for w in range(wins)]
    rolled = 0
    for r in range(ROUNDS):
        for w in range(wins):
            if r >= SLACK:
                arrived(w, r - SLACK)
                for i in range(STREAMS):
                    value = held[w][r - SLACK][forward[w][i]]
                    if r < CHUNKS:
                        value = jnp.where(root[w], own[rows_of(w, r, i), :], value)
                    sent[w][r][i] = value
            for i in range(STREAMS):
                pltpu.make_async_remote_copy(
                    src_ref=sent[w][r].at[i] if r >= SLACK else own.at[rows_of(w, min(r, CHUNKS - 1), i), :],
                    dst_ref=held[w][r].at[i],
                    send_sem=send_sem.at[w, r],
                    recv_sem=recv_sem.at[w, r],
                    device_id=partner(i),
                    device_id_type=MESH,
                ).start()
        if r == 0:
            a_scatter()
        if r == A_GATHER:
            a_gather()
        if r == A_ROLL:
            a_wait(a_recv, 1, a_all)
        if r >= A_ROLL:
            upto = FINE * (r - A_ROLL + 1) // (ROUNDS - A_ROLL)
            for k in range(rolled, upto):
                roll_part(k)
            rolled = upto

    slot = [[routes[row[w] + STREAMS + j] for j in range(STREAMS)] for w in range(wins)]
    step = [[routes[row[w] + 2 * STREAMS + j] for j in range(STREAMS)] for w in range(wins)]
    last = (STEPS - 1) * SLACK
    bt[pl.ds(wins * samples, LAGS), :] = jnp.zeros((LAGS, rcv), jnp.bfloat16)
    for r in range(max(0, ROUNDS - SLACK), last):
        for w in range(wins):
            arrived(w, r)
    scale = 1.0 / (float((samples - LAGS) * wins) ** 0.5)
    group = lax.broadcasted_iota(jnp.int32, (1, LAGS), 1) // BLOCK
    factor = jnp.zeros((1, LAGS), jnp.float32)
    for g in range(LAGS // BLOCK):
        factor = jnp.where(group == g, active[0, g].astype(jnp.float32) * scale, factor)

    def product(start, stop, first, final):
        def pair_step(pair, carry):
            base = pl.multiple_of(pair * 2 * FINE, FINE)
            left, right = [], []
            for w in range(wins):
                both = [bt[pl.ds(base + (w * samples + start + FINE * jj), stop - start), :] for jj in range(2)]
                right.append(jnp.concatenate(both, axis=1))
                left.append(toep[:, w * samples + start : w * samples + stop])
            part = jnp.dot(
                jnp.concatenate(left, axis=1), jnp.concatenate(right, axis=0), preferred_element_type=jnp.float32
            )
            columns = pl.ds(pl.multiple_of(pair * 256, 256), 256)
            if not first:
                part = part + acc[:, columns]
            if not final:
                acc[:, columns] = part
            else:
                for jj in range(2):
                    for k in range(FINE):
                        lagged[pl.ds(base + FINE * jj + k, src, stride=LAGS), :] = (
                            part[k * src : (k + 1) * src, jj * LAGS : (jj + 1) * LAGS] * factor
                        )
            return carry

        lax.fori_loop(0, LAGS // FINE // 2, pair_step, 0)

    done = 0
    for c in range(CHUNKS):
        for w in range(wins):
            if c + last >= ROUNDS - SLACK:
                arrived(w, c + last)
            for j in range(STREAMS):
                value = own[rows_of(w, c, j), :]
                for d in range(1, STEPS + 1):
                    value = jnp.where(step[w][j] == d, held[w][c + (d - 1) * SLACK][slot[w][j]], value)
                bt[rows_of(w, c, j), :] = value
        if c + 1 in PASSES:
            stop = samples if c == CHUNKS - 1 else (c + 1) * STREAMS * piece - LAGS
            product(done, stop, done == 0, c == CHUNKS - 1)
            done = stop

    a_wait(a_send, 0, a_all)
    a_wait(a_send, 1, a_all)
    for r in range(ROUNDS):
        for w in range(wins):
            pltpu.make_async_copy(held[w][r], held[w][r], send_sem.at[w, r]).wait()


def spread(src_owner, rcv_owner, active, src_traces, rcv_traces, peers):
    wins, _, src, samples = src_traces.shape
    rcv = rcv_traces.shape[2]
    routes = jnp.asarray(np.array(ROUTES, np.int32).reshape(-1))
    piece = samples // (CHUNKS * STREAMS)
    parts = pltpu.VMEM((peers, wins, src, samples // peers), jnp.bfloat16)
    anywhere = pl.BlockSpec(memory_space=pl.ANY)
    operands = (routes, src_owner.T, rcv_owner.T, active, src_traces, rcv_traces)
    operands = [pltpu.with_memory_space_constraint(v, pltpu.HBM) for v in operands]
    return pl.pallas_call(
        spread_kernel,
        out_shape=jax.ShapeDtypeStruct((src * LAGS, rcv), jnp.float32),
        in_specs=[anywhere] * 6,
        out_specs=pl.BlockSpec(memory_space=pltpu.VMEM),
        scratch_shapes=[
            pltpu.SMEM(routes.shape, jnp.int32),
            pltpu.SMEM((1, wins), jnp.int32),
            pltpu.SMEM((1, wins), jnp.int32),
            pltpu.SMEM(active.shape, jnp.int32),
            pltpu.VMEM(src_traces.shape, jnp.bfloat16),
            pltpu.VMEM(rcv_traces.shape, jnp.bfloat16),
            parts,
            parts,
            parts,
            pltpu.VMEM((wins * samples, rcv), jnp.bfloat16),
            pltpu.VMEM((wins * samples + LAGS, rcv), jnp.bfloat16),
            pltpu.VMEM((FINE * src, wins * samples), jnp.bfloat16),
            pltpu.VMEM((FINE * src, rcv * LAGS // FINE), jnp.float32),
            pltpu.SemaphoreType.DMA((wins + 5,)),
            pltpu.SemaphoreType.DMA((wins, ROUNDS)),
            pltpu.SemaphoreType.DMA((wins, ROUNDS)),
            pltpu.SemaphoreType.DMA((2,)),
            pltpu.SemaphoreType.DMA((2,)),
        ]
        + [pltpu.VMEM((STREAMS, piece, rcv), jnp.bfloat16)] * (2 * wins * ROUNDS),
        compiler_params=pltpu.CompilerParams(collective_id=0, has_side_effects=True, vmem_limit_bytes=48 * 2**20),
    )(*operands)


def finish_kernel(lagged, out_hbm, out_v, sem):
    src = out_v.shape[0]
    for s in range(src):
        out_v[s] = lagged[s * LAGS : (s + 1) * LAGS, :].T
        if s % 4 == 3:
            part = pl.ds(s - 3, 4)
            pltpu.make_async_copy(out_v.at[part], out_hbm.at[part], sem.at[s // 4]).start()
    for q in range(src // 4):
        part = pl.ds(q * 4, 4)
        pltpu.make_async_copy(out_v.at[part], out_hbm.at[part], sem.at[q]).wait()


def finish(lagged):
    rows, rcv = lagged.shape
    src = rows // LAGS
    return pl.pallas_call(
        finish_kernel,
        out_shape=jax.ShapeDtypeStruct((src, rcv, LAGS), jnp.float32),
        in_specs=[pl.BlockSpec(memory_space=pltpu.VMEM)],
        out_specs=pl.BlockSpec(memory_space=pl.ANY),
        scratch_shapes=[pltpu.VMEM((src, rcv, LAGS), jnp.float32), pltpu.SemaphoreType.DMA((src // 4,))],
        compiler_params=pltpu.CompilerParams(vmem_limit_bytes=16 * 2**20),
    )(lagged)


def solution(mesh):
    peers = mesh.shape["rcv"]

    def body(src_traces, rcv_traces, src_owner, rcv_owner, active):
        return finish(spread(src_owner, rcv_owner, active, src_traces, rcv_traces, peers))

    return jax.shard_map(
        body,
        mesh=mesh,
        in_specs=(
            P(None, "rcv", "src", None),
            P(None, "src", "rcv", None),
            P(None, "src"),
            P(None, "rcv"),
            P("src", "rcv"),
        ),
        out_specs=P("src", "rcv", None),
        check_vma=False,
    )
```

time: 53.2 us -> 41.2 us (0.77)
  the two profiles are of different devices: /device:TPU:1 before, /device:TPU:6 now
where the time goes in v2:
time: 41.2 us; the launch traced here: 41.1 us
  Pallas kernels  41.1 us (100%)
    pallas_call x1, Pallas kernels, spread(): pl.pallas_call(spread_kernel, out_shape=jax.ShapeDtypeStruct((src * LAGS,...  39.6 us
    pallas_call x1, Pallas kernels, finish(): pl.pallas_call(finish_kernel, out_shape=jax.ShapeDtypeStruct((src, rcv, L...  1.51 us

profile of v2, /device:TPU:6, one launch (start us, length us, event | category | flops | bytes accessed | tf_op | source)
XLA Modules:
  0.0 41.1 jit_solution(9993357109386859368)
XLA Ops:
  0.0 39.6 %shard_map.64.lagged = f32[4096,128]{1,0:T(8,128)S(1)} custom-call(s32[768]{0:T(1024)} %constant.2.clone.routes_hbm, s32[1,2]{1,0:T(1,128)} %bitcast.2, s32[1,2]{1,0:T(1,128)} %bitcast.3, s32[1,4]{1,0:T(1,128)} %active_hbm.1, bf16[2,1,32,2048]{3,2,1,0:T(8,128)(2,1)} %src_hbm.1, bf16[2,1,128,2048]{3,2,1,0:T(8,128)(2,1)} %rcv_hbm.1), custom_call_target="tpu_custom_call" | custom-call | tf_op jit(solution)/shard_map/pallas_call | solution.py:276
  39.6 1.5 %shard_map.65 = f32[32,128,128]{2,1,0:T(8,128)} custom-call(f32[4096,128]{1,0:T(8,128)S(1)} %shard_map.64.lagged), custom_call_target="tpu_custom_call" | custom-call | tf_op jit(solution)/shard_map/pallas_call | solution.py:321

commit v3 on v2

--- a/solution.py
+++ b/solution.py
@@ -17,9 +17,9 @@
 CHUNKS = 8
 STEPS = 4
 SLACK = 4
-A_GATHER = 4
-A_ROLL = 12
-PASSES = (4, 6, 8)
+A_GATHER = 5
+A_ROLL = 11
+PASSES = (5, 8)
 ROUNDS = CHUNKS + (STEPS - 1) * SLACK
 ROUTES = (
     (0, 0, 0, 0, 0, 0, 0, 0, 0, 0, 0, 0, 0, 0, 0, 0, 0, 0, 0, 0, 0, 0, 0, 0),
@@ -103,16 +103,21 @@
         load.start()
 
     width = samples // (others + 1)
-    for w in range(wins):
+
+    def ready_receivers(w):
         loads[w].wait()
         rows = normalised(rcv_ref[w, 0].astype(jnp.float32))
         for t in range(samples // LAGS):
             own[pl.ds(w * samples + t * LAGS, LAGS), :] = rows[:, t * LAGS : (t + 1) * LAGS].T.astype(jnp.bfloat16)
-    loads[wins].wait()
-    for w in range(wins):
-        rows = normalised(src_ref[w, 0].astype(jnp.float32)).astype(jnp.bfloat16)
-        for i in range(others + 1):
-            a_own[i, w] = rows[:, i * width : (i + 1) * width]
+
+    def ready_sources():
+        loads[wins].wait()
+        for w in range(wins):
+            rows = normalised(src_ref[w, 0].astype(jnp.float32)).astype(jnp.bfloat16)
+            for i in range(others + 1):
+                a_own[i, w] = rows[:, i * width : (i + 1) * width]
+
+    ready_receivers(0)
     for load in loads[wins + 1 :]:
         load.wait()
     pl.semaphore_wait(barrier, len(seen) + others)
@@ -175,6 +180,8 @@
     rolled = 0
     for r in range(ROUNDS):
         for w in range(wins):
+            if r == 0 and w > 0:
+                ready_receivers(w)
             if r >= SLACK:
                 arrived(w, r - SLACK)
                 for i in range(STREAMS):
@@ -191,7 +198,8 @@
                     device_id=partner(i),
                     device_id_type=MESH,
                 ).start()
-        if r == 0:
+        if r == 1:
+            ready_sources()
             a_scatter()
         if r == A_GATHER:
             a_gather()

time: 41.2 us -> 40.6 us (0.985)
  Pallas kernels: 41.1 us -> 40.4 us
    pallas_call x1, Pallas kernels: 39.6 us -> 38.9 us  [spread(): pl.pallas_call(spread_kernel, out_shape=jax.ShapeDtypeStruct((src * LAGS,...]
where the time goes in v3:
time: 40.6 us; the launch traced here: 40.5 us
  Pallas kernels  40.4 us (100%)
    pallas_call x1, Pallas kernels, spread(): pl.pallas_call(spread_kernel, out_shape=jax.ShapeDtypeStruct((src * LAGS,...  38.9 us
    pallas_call x1, Pallas kernels, finish(): pl.pallas_call(finish_kernel, out_shape=jax.ShapeDtypeStruct((src, rcv, L...  1.51 us

profile of v3, /device:TPU:6, one launch (start us, length us, event | category | flops | bytes accessed | tf_op | source)
XLA Modules:
  0.0 40.5 jit_solution(824882593240656440)
XLA Ops:
  0.0 38.9 %shard_map.64.lagged = f32[4096,128]{1,0:T(8,128)S(1)} custom-call(s32[768]{0:T(1024)} %constant.2.clone.routes_hbm, s32[1,2]{1,0:T(1,128)} %bitcast.2, s32[1,2]{1,0:T(1,128)} %bitcast.3, s32[1,4]{1,0:T(1,128)} %active_hbm.1, bf16[2,1,32,2048]{3,2,1,0:T(8,128)(2,1)} %src_hbm.1, bf16[2,1,128,2048]{3,2,1,0:T(8,128)(2,1)} %rcv_hbm.1), custom_call_target="tpu_custom_call" | custom-call | tf_op jit(solution)/shard_map/pallas_call | solution.py:284
  38.9 1.5 %shard_map.65 = f32[32,128,128]{2,1,0:T(8,128)} custom-call(f32[4096,128]{1,0:T(8,128)S(1)} %shard_map.64.lagged), custom_call_target="tpu_custom_call" | custom-call | tf_op jit(solution)/shard_map/pallas_call | solution.py:329

commit v4 on v3

--- a/solution.py
+++ b/solution.py
@@ -1,3 +1,5 @@
+import functools
+
 import jax
 import jax.numpy as jnp
 import numpy as np
@@ -19,7 +21,7 @@
 SLACK = 4
 A_GATHER = 5
 A_ROLL = 11
-PASSES = (5, 8)
+PASSES = (4, 8)
 ROUNDS = CHUNKS + (STEPS - 1) * SLACK
 ROUTES = (
     (0, 0, 0, 0, 0, 0, 0, 0, 0, 0, 0, 0, 0, 0, 0, 0, 0, 0, 0, 0, 0, 0, 0, 0),
@@ -66,8 +68,8 @@
 
 def spread_kernel(
     routes_hbm, src_owner_hbm, rcv_owner_hbm, active_hbm, src_hbm, rcv_hbm,
-    lagged,
-    routes, src_owner, rcv_owner, active, src_ref, rcv_ref, a_own, a_cand, a_all, own, bt, toep, acc,
+    acc,
+    routes, src_owner, rcv_owner, active, src_ref, rcv_ref, a_own, a_cand, a_all, own, bt, toep,
     load_sem, send_sem, recv_sem, a_send, a_recv,
     *rest,
 ):
@@ -173,8 +175,27 @@
         for w in range(wins):
             a = jnp.concatenate([a_all[i, w] for i in range(others + 1)], axis=1).astype(jnp.float32)
             a = jnp.where(lane < samples - LAGS, a, 0.0)
-            rolled = a if k == 0 else pltpu.roll(a, k, 1)
+            rolled = pltpu.roll(a, LAGS - FINE + k, 1)
             toep[pl.ds(k * src, src), w * samples : (w + 1) * samples] = rolled.astype(jnp.bfloat16)
+
+    slot = [[routes[row[w] + STREAMS + j] for j in range(STREAMS)] for w in range(wins)]
+    step = [[routes[row[w] + 2 * STREAMS + j] for j in range(STREAMS)] for w in range(wins)]
+    last = (STEPS - 1) * SLACK
+
+    deep = LAGS + samples
+    group = lax.broadcasted_iota(jnp.int32, (1, rcv), 1) // BLOCK
+    listed = jnp.zeros((1, rcv), jnp.float32)
+    for g in range(rcv // BLOCK):
+        listed = jnp.where(group == g, active[0, g].astype(jnp.float32), listed)
+    listed = listed.astype(jnp.bfloat16)
+
+    def gather_chunk(c):
+        for w in range(wins):
+            for j in range(STREAMS):
+                value = own[rows_of(w, c, j), :]
+                for d in range(1, STEPS + 1):
+                    value = jnp.where(step[w][j] == d, held[w][c + (d - 1) * SLACK][slot[w][j]], value)
+                bt[pl.ds(w * deep + LAGS + (c * STREAMS + j) * piece, piece), :] = value * listed
 
     forward = [[routes[row[w] + i] for i in range(STREAMS)] for w in range(wins)]
     rolled = 0
@@ -198,6 +219,10 @@
                     device_id=partner(i),
                     device_id_type=MESH,
                 ).start()
+        if r == 2:
+            acc[...] = jnp.zeros_like(acc)
+            for w in range(wins):
+                bt[pl.ds(w * deep, LAGS), :] = jnp.zeros((LAGS, rcv), jnp.bfloat16)
         if r == 1:
             ready_sources()
             a_scatter()
@@ -210,66 +235,41 @@
             for k in range(rolled, upto):
                 roll_part(k)
             rolled = upto
-
-    slot = [[routes[row[w] + STREAMS + j] for j in range(STREAMS)] for w in range(wins)]
-    step = [[routes[row[w] + 2 * STREAMS + j] for j in range(STREAMS)] for w in range(wins)]
-    last = (STEPS - 1) * SLACK
-    bt[pl.ds(wins * samples, LAGS), :] = jnp.zeros((LAGS, rcv), jnp.bfloat16)
-    for r in range(max(0, ROUNDS - SLACK), last):
-        for w in range(wins):
-            arrived(w, r)
-    scale = 1.0 / (float((samples - LAGS) * wins) ** 0.5)
-    group = lax.broadcasted_iota(jnp.int32, (1, LAGS), 1) // BLOCK
-    factor = jnp.zeros((1, LAGS), jnp.float32)
-    for g in range(LAGS // BLOCK):
-        factor = jnp.where(group == g, active[0, g].astype(jnp.float32) * scale, factor)
-
-    def product(start, stop, first, final):
-        def pair_step(pair, carry):
-            base = pl.multiple_of(pair * 2 * FINE, FINE)
-            left, right = [], []
-            for w in range(wins):
-                both = [bt[pl.ds(base + (w * samples + start + FINE * jj), stop - start), :] for jj in range(2)]
-                right.append(jnp.concatenate(both, axis=1))
-                left.append(toep[:, w * samples + start : w * samples + stop])
-            part = jnp.dot(
-                jnp.concatenate(left, axis=1), jnp.concatenate(right, axis=0), preferred_element_type=jnp.float32
-            )
-            columns = pl.ds(pl.multiple_of(pair * 256, 256), 256)
-            if not first:
-                part = part + acc[:, columns]
-            if not final:
-                acc[:, columns] = part
-            else:
-                for jj in range(2):
-                    for k in range(FINE):
-                        lagged[pl.ds(base + FINE * jj + k, src, stride=LAGS), :] = (
-                            part[k * src : (k + 1) * src, jj * LAGS : (jj + 1) * LAGS] * factor
-                        )
-            return carry
-
-        lax.fori_loop(0, LAGS // FINE // 2, pair_step, 0)
-
-    done = 0
-    for c in range(CHUNKS):
-        for w in range(wins):
-            if c + last >= ROUNDS - SLACK:
-                arrived(w, c + last)
-            for j in range(STREAMS):
-                value = own[rows_of(w, c, j), :]
-                for d in range(1, STEPS + 1):
-                    value = jnp.where(step[w][j] == d, held[w][c + (d - 1) * SLACK][slot[w][j]], value)
-                bt[rows_of(w, c, j), :] = value
-        if c + 1 in PASSES:
-            stop = samples if c == CHUNKS - 1 else (c + 1) * STREAMS * piece - LAGS
-            product(done, stop, done == 0, c == CHUNKS - 1)
-            done = stop
-
-    a_wait(a_send, 0, a_all)
-    a_wait(a_send, 1, a_all)
-    for r in range(ROUNDS):
-        for w in range(wins):
-            pltpu.make_async_copy(held[w][r], held[w][r], send_sem.at[w, r]).wait()
+        if r - SLACK >= last:
+            gather_chunk(r - SLACK - last)
+
+    half = samples // 2
+
+    def part_step(at, carry):
+        late, pair = at // 4, at % 4
+
+        @pl.when(at == 4)
+        def _():
+            for c in range(CHUNKS - SLACK, CHUNKS):
+                for w in range(wins):
+                    arrived(w, c + last)
+                gather_chunk(c)
+            a_wait(a_send, 0, a_all)
+            a_wait(a_send, 1, a_all)
+            for r in range(ROUNDS):
+                for w in range(wins):
+                    pltpu.make_async_copy(held[w][r], held[w][r], send_sem.at[w, r]).wait()
+
+        start = pl.multiple_of(late * half, half)
+        base = pl.multiple_of(late * half + pair * 2 * FINE, FINE)
+        left, right = [], []
+        for w in range(wins):
+            both = [bt[pl.ds(base + (w * deep + FINE + FINE * jj), half), :] for jj in range(2)]
+            right.append(jnp.concatenate(both, axis=1))
+            left.append(toep[:, pl.ds(pl.multiple_of(w * samples + start, half), half)])
+        part = jnp.dot(
+            jnp.concatenate(left, axis=1), jnp.concatenate(right, axis=0), preferred_element_type=jnp.float32
+        )
+        for jj in range(2):
+            acc[2 * pair + jj] += part[:, jj * rcv : (jj + 1) * rcv]
+        return carry
+
+    lax.fori_loop(0, 8, part_step, 0)
 
 
 def spread(src_owner, rcv_owner, active, src_traces, rcv_traces, peers):
@@ -283,7 +283,7 @@
     operands = [pltpu.with_memory_space_constraint(v, pltpu.HBM) for v in operands]
     return pl.pallas_call(
         spread_kernel,
-        out_shape=jax.ShapeDtypeStruct((src * LAGS, rcv), jnp.float32),
+        out_shape=jax.ShapeDtypeStruct((LAGS // FINE, FINE * src, rcv), jnp.float32),
         in_specs=[anywhere] * 6,
         out_specs=pl.BlockSpec(memory_space=pltpu.VMEM),
         scratch_shapes=[
@@ -297,9 +297,8 @@
             parts,
             parts,
             pltpu.VMEM((wins * samples, rcv), jnp.bfloat16),
-            pltpu.VMEM((wins * samples + LAGS, rcv), jnp.bfloat16),
+            pltpu.VMEM((wins * (samples + LAGS), rcv), jnp.bfloat16),
             pltpu.VMEM((FINE * src, wins * samples), jnp.bfloat16),
-            pltpu.VMEM((FINE * src, rcv * LAGS // FINE), jnp.float32),
             pltpu.SemaphoreType.DMA((wins + 5,)),
             pltpu.SemaphoreType.DMA((wins, ROUNDS)),
             pltpu.SemaphoreType.DMA((wins, ROUNDS)),
@@ -311,10 +310,11 @@
     )(*operands)
 
 
-def finish_kernel(lagged, out_hbm, out_v, sem):
+def finish_kernel(scale, acc, out_hbm, out_v, sem):
     src = out_v.shape[0]
     for s in range(src):
-        out_v[s] = lagged[s * LAGS : (s + 1) * LAGS, :].T
+        lags = [acc[j, pl.ds(s, FINE, stride=src), :] for j in range(LAGS // FINE)]
+        out_v[s] = (jnp.concatenate(lags, axis=0) * scale).T
         if s % 4 == 3:
             part = pl.ds(s - 3, 4)
             pltpu.make_async_copy(out_v.at[part], out_hbm.at[part], sem.at[s // 4]).start()
@@ -323,24 +323,26 @@
         pltpu.make_async_copy(out_v.at[part], out_hbm.at[part], sem.at[q]).wait()
 
 
-def finish(lagged):
-    rows, rcv = lagged.shape
-    src = rows // LAGS
+def finish(acc, scale):
+    _, rows, rcv = acc.shape
+    src = rows // FINE
     return pl.pallas_call(
-        finish_kernel,
+        functools.partial(finish_kernel, scale),
         out_shape=jax.ShapeDtypeStruct((src, rcv, LAGS), jnp.float32),
         in_specs=[pl.BlockSpec(memory_space=pltpu.VMEM)],
         out_specs=pl.BlockSpec(memory_space=pl.ANY),
         scratch_shapes=[pltpu.VMEM((src, rcv, LAGS), jnp.float32), pltpu.SemaphoreType.DMA((src // 4,))],
         compiler_params=pltpu.CompilerParams(vmem_limit_bytes=16 * 2**20),
-    )(lagged)
+    )(acc)
 
 
 def solution(mesh):
     peers = mesh.shape["rcv"]
 
     def body(src_traces, rcv_traces, src_owner, rcv_owner, active):
-        return finish(spread(src_owner, rcv_owner, active, src_traces, rcv_traces, peers))
+        wins, _, _, samples = src_traces.shape
+        scale = 1.0 / (float((samples - LAGS) * wins) ** 0.5)
+        return finish(spread(src_owner, rcv_owner, active, src_traces, rcv_traces, peers), scale)
 
     return jax.shard_map(
         body,

time: 40.6 us -> 40.2 us (level)
    pallas_call x2, Pallas kernels: 40.4 us -> 40 us  [the longest x1 37.9 us: spread(): pl.pallas_call(spread_kernel, out_shape=jax.ShapeDtypeStruct((LAGS // FIN...]
where the time goes in v4:
time: 40.2 us; the launch traced here: 40 us
  Pallas kernels  40 us (100%)
    pallas_call x1, Pallas kernels, spread(): pl.pallas_call(spread_kernel, out_shape=jax.ShapeDtypeStruct((LAGS // FIN...  37.9 us
    pallas_call x1, Pallas kernels, finish(): pl.pallas_call(functools.partial(finish_kernel, scale), out_shape=jax.Sha...  2.11 us

profile of v4, /device:TPU:6, one launch (start us, length us, event | category | flops | bytes accessed | tf_op | source)
XLA Modules:
  0.0 40.0 jit_solution(15274341169211344798)
XLA Ops:
  0.0 37.9 %shard_map.64.acc = f32[8,512,128]{2,1,0:T(8,128)S(1)} custom-call(s32[768]{0:T(1024)} %constant.2.clone.routes_hbm, s32[1,2]{1,0:T(1,128)} %bitcast.2, s32[1,2]{1,0:T(1,128)} %bitcast.3, s32[1,4]{1,0:T(1,128)} %active_hbm.1, bf16[2,1,32,2048]{3,2,1,0:T(8,128)(2,1)} %src_hbm.1, bf16[2,1,128,2048]{3,2,1,0:T(8,128)(2,1)} %rcv_hbm.1), custom_call_target="tpu_custom_call" | custom-call | tf_op jit(solution)/shard_map/pallas_call | solution.py:284
  37.9 2.1 %shard_map.65 = f32[32,128,128]{2,1,0:T(8,128)} custom-call(f32[8,512,128]{2,1,0:T(8,128)S(1)} %shard_map.64.acc), custom_call_target="tpu_custom_call" | custom-call | tf_op jit(solution)/shard_map/pallas_call | solution.py:329
